TPU v7x, 512 devices: a whole 4x4x16 slice. The times are simulated.
512 devices in a mesh: expert: 32 (over x_lo, z), tensor: 16 (over y, x_hi, core).
Axes of the slice: x: 4 (x_hi: 2, x_lo: 2; x = x_hi * 2 + x_lo), y: 4, z: 16, core: 2. Of those that a mesh axis runs over, the one named last changes fastest.
Arguments:
- tokens: bfloat16 [1536, 5120], P('expert', 'tensor'), may hold values from -6 to 6
- expert_ids: int32 [1536, 6], P('expert'), may hold values from 0 to 31, all different within a row; in each aligned block of 48 rows (0 to 47, 48 to 95, ...) at most 18 rows name the same one
- route_weights: float32 [1536, 6], P('expert'), may hold values from 0.05 to 0.6
- routed_gate: bfloat16 [32, 1536, 5120], P('expert', 'tensor'), may hold values from -0.078125 to 0.078125
- routed_up: bfloat16 [32, 1536, 5120], P('expert', 'tensor'), may hold values from -0.078125 to 0.078125
- routed_down: bfloat16 [32, 1536, 5120], P('expert', None, 'tensor'), may hold values from -0.15625 to 0.15625
- shared_gate: bfloat16 [5120, 3072], P('expert', 'tensor'), may hold values from -0.078125 to 0.078125
- shared_up: bfloat16 [5120, 3072], P('expert', 'tensor'), may hold values from -0.078125 to 0.078125
- shared_down: bfloat16 [3072, 5120], P('tensor', 'expert'), may hold values from -0.21875 to 0.21875
- norm_gain: float32 [5120], replicated, may hold values from 0.25 to 1.75
- proj_weight: bfloat16 [2112, 5120], P('tensor'), may hold values from -0.078125 to 0.078125
Outputs:
- stream: bfloat16 [1536, 5120], P('expert', 'tensor')
- projected: bfloat16 [1536, 2112], P('expert', 'tensor')
Inputs may be any that keep to these rules, and one draw needn't show every extreme that they name: `expert_ids`: in each aligned block of 48 tokens (those of one index of expert) no expert is chosen by more than 18 tokens, and some expert is chosen by exactly 18; a token's 6 experts differ.
All inputs are finite; a program needn't handle non-finite values.
Results may differ from a plain program's by a relative error of at most 0.019.
Values may be sent and summed in bfloat16 or wider, within the bound.
No kernel may reach another device: no remote copies, remote signals or barrier semaphores. Data moves between devices by JAX's collectives and lax.ppermute only.
A program may use at most 128 MiB of HBM per device.

v0:
```python
import jax
import jax.numpy as jnp
from jax import lax
from jax.sharding import PartitionSpec as P


def swiglu(gate, up):
    return (jax.nn.silu(gate) * up).astype(jnp.bfloat16)


def dot_rows(left, right):
    return lax.dot_general(
        left, right, (((1,), (1,)), ((), ())), preferred_element_type=jnp.float32
    )


def per_device(
    tokens,
    expert_ids,
    route_weights,
    routed_gate,
    routed_up,
    routed_down,
    shared_gate,
    shared_up,
    shared_down,
    norm_gain,
    proj_weight,
):
    tok_rows = tokens.shape[0]
    local_width = tokens.shape[1]
    top = expert_ids.shape[1]
    experts = lax.axis_size("expert")
    capacity = min(tok_rows, 2 * tok_rows * top // experts)
    features = lax.all_gather(tokens, "tensor", axis=1, tiled=True)
    flat_ids = expert_ids.reshape(-1)
    onehot = (flat_ids[:, None] == jnp.arange(experts, dtype=jnp.int32)[None, :]).astype(jnp.int32)
    slots = jnp.sum((jnp.cumsum(onehot, axis=0) - onehot) * onehot, axis=1)
    target = flat_ids * capacity + slots
    owners = jnp.repeat(jnp.arange(tok_rows, dtype=jnp.int32), top)
    sources = jnp.full((experts * capacity,), tok_rows, jnp.int32).at[target].set(owners)
    gate_w = routed_gate[0]
    up_w = routed_up[0]
    down_w = routed_down[0]
    padded = jnp.concatenate([features, jnp.zeros((1, features.shape[1]), features.dtype)], axis=0)
    outgoing = padded[sources].reshape(experts, capacity, features.shape[1])
    arrived = lax.all_to_all(outgoing, "expert", split_axis=0, concat_axis=0, tiled=True)
    count = arrived.shape[1]
    rows = arrived.reshape(-1, arrived.shape[2])
    hidden = swiglu(dot_rows(rows, gate_w), dot_rows(rows, up_w))
    hidden_all = lax.all_gather(hidden, "tensor", axis=1, tiled=True)
    result = jnp.dot(hidden_all, down_w, preferred_element_type=jnp.float32).astype(jnp.bfloat16)
    result = result.reshape(experts, count, result.shape[1])
    returned = lax.all_to_all(result, "expert", split_axis=0, concat_axis=0, tiled=True)
    flat_back = returned.reshape(experts * capacity, returned.shape[2])
    picked = flat_back[target].reshape(tok_rows, top, returned.shape[2]).astype(jnp.float32)
    routed = jnp.sum(picked * route_weights[:, :, None], axis=1)
    gate_sum = jnp.dot(
        features,
        lax.all_gather(shared_gate, "expert", axis=0, tiled=True),
        preferred_element_type=jnp.float32,
    )
    up_sum = jnp.dot(
        features,
        lax.all_gather(shared_up, "expert", axis=0, tiled=True),
        preferred_element_type=jnp.float32,
    )
    shared_hidden = swiglu(gate_sum, up_sum)
    shared_terms = jnp.dot(
        shared_hidden,
        lax.all_gather(shared_down, "expert", axis=1, tiled=True),
        preferred_element_type=jnp.float32,
    )
    rank = lax.axis_index("tensor")
    shared_full = lax.psum(shared_terms.astype(jnp.bfloat16), "tensor").astype(jnp.float32)
    shared_mine = lax.dynamic_slice_in_dim(shared_full, rank * local_width, local_width, 1)
    stream = (tokens.astype(jnp.float32) + shared_mine + routed).astype(jnp.bfloat16)
    stream_all = lax.all_gather(stream, "tensor", axis=1, tiled=True)
    values = stream_all.astype(jnp.float32)
    scale = lax.rsqrt(jnp.mean(values * values, axis=1, keepdims=True) + 1e-06)
    normed = (values * scale * norm_gain[None, :]).astype(jnp.bfloat16)
    projected = dot_rows(normed, proj_weight).astype(jnp.bfloat16)
    return (stream, projected)


def solution(mesh):
    in_specs = (
        P("expert", "tensor"),
        P("expert", None),
        P("expert", None),
        P("expert", "tensor", None),
        P("expert", "tensor", None),
        P("expert", None, "tensor"),
        P("expert", "tensor"),
        P("expert", "tensor"),
        P("tensor", "expert"),
        P(),
        P("tensor", None),
    )
    out_specs = (P("expert", "tensor"), P("expert", "tensor"))
    return jax.shard_map(
        per_device, mesh=mesh, in_specs=in_specs, out_specs=out_specs, check_vma=False
    )
```

profile of v0, /device:TPU:1, one launch (start us, length us, event | category | flops | bytes accessed | tf_op | source)
XLA Modules:
  0.0 1078.2 jit_solution(14754052590517255412)
XLA Ops:
  7.2 0.0 copy-start
  7.2 0.0 all-gather.13.cloned.1.call-start
  7.2 0.9 copy.26
  8.1 0.7 broadcast_multiply_fusion
  8.8 0.1 eq.22
  8.9 0.9 reduce-window.6
  9.8 0.2 slice_reduce_fusion
  10.1 0.1 bitcast_bitcast_fusion
  10.2 0.1 copy.25
  10.3 0.1 mul.68
  10.4 0.1 reshape.102
  10.6 2.9 scatter_custom_fusion
  13.5 29.4 %all-gather = bf16[16,320,48]{1,2,0:T(8,128)(2,1)S(1)} all-gather(bf16[1,320,48]{1,2,0:T(8,128)(2,1)} %bitcast.43), channel_id=1, replica_groups=mesh['expert'=32,'tensor'=16] {'tensor'}, dimensions={0}, use_global_device_ids=true | all-gather | bytes 522240 | tf_op jit(solution)/shard_map/all_gather | solution.py:35
  43.0 0.1 copy.24
  43.1 0.4 reshape.108
  43.6 6.0 gather_fusion
  49.6 8.5 reshape.76
  58.1 359.3 %all_to_all.10 = bf16[32,18,5120]{2,1,0:T(8,128)(2,1)} all-to-all(bf16[32,18,5120]{2,1,0:T(8,128)(2,1)} %reshape.76), channel_id=1, replica_groups=mesh['expert'=32,'tensor'=16] {'expert'}, dimensions={0} | all-to-all | bytes 11796480 | tf_op jit(solution)/shard_map/all_to_all | solution.py:47
  417.4 0.0 copy-start.2
  417.4 8.8 reshape.77
  426.2 0.0 copy-done.2
  426.2 0.0 copy-start.1
  426.2 4.8 fusion.4
  431.0 0.0 copy-done.1
  431.0 0.0 copy-done.6
  431.1 2.6 fusion
  433.7 0.0 all-gather.13.cloned.1.call-update
  433.7 0.0 all-gather.7.cloned.1.call-start
  433.8 0.7 all-gather.7.cloned.1.call-update
  434.5 0.0 all-gather.11.cloned.1.call-start
  434.5 0.7 all-gather.11.cloned.1.call-update
  435.2 0.0 all-gather.9.cloned.1.call-start
  435.3 0.5 all-gather.9.cloned.1.call-update
  435.8 51.4 %all-gather.13.cloned.1.call-done = bf16[576,1536]{0,1:T(8,128)(2,1)} async-done(((bf16[576,96]{0,1:T(8,128)(2,1)}), bf16[576,1536]{0,1:T(8,128)(2,1)}) %all-gather.13.cloned.1.call-update) | async-done | bytes 1769488 | tf_op jit(solution)/shard_map/all_gather | solution.py:51
  487.2 2.8 convolution_convert_fusion.1
  490.0 0.2 copy.29
  490.2 1.0 reshape.78
  491.3 12.3 %all-to-all-start.1 = ((bf16[32,18,320]{2,1,0:T(8,128)(2,1)}), bf16[32,18,320]{2,1,0:T(8,128)(2,1)S(1)}, u32[]{:S(2)}, u32[]{:S(2)}) async-start(bf16[32,18,320]{2,1,0:T(8,128)(2,1)} %reshape.78), calls=%async_computation.1 | async-start | bytes 1179648 | tf_op jit(solution)/shard_map/all_to_all | solution.py:54
  503.6 0.2 all-reduce.4.cloned.1.call-start
  503.8 110.9 %all-gather.7.cloned.1.call-done = bf16[5120,192]{1,0:T(8,128)(2,1)} async-done(((bf16[160,192]{1,0:T(8,128)(2,1)}), bf16[5120,192]{1,0:T(8,128)(2,1)}) %all-gather.7.cloned.1.call-update) | async-done | bytes 1966096 | tf_op jit(solution)/shard_map/all_gather | solution.py:60
  614.7 2.3 fusion.20
  617.0 0.0 copy-start.5
  617.0 123.6 %all-gather.11.cloned.1.call-done = bf16[192,5120]{0,1:T(8,128)(2,1)} async-done(((bf16[192,160]{0,1:T(8,128)(2,1)}), bf16[192,5120]{0,1:T(8,128)(2,1)}) %all-gather.11.cloned.1.call-update) | async-done | bytes 1966096 | tf_op jit(solution)/shard_map/all_gather | solution.py:71
  740.7 130.1 %all-gather.9.cloned.1.call-done = bf16[5120,192]{1,0:T(8,128)(2,1)} async-done(((bf16[160,192]{1,0:T(8,128)(2,1)}), bf16[5120,192]{1,0:T(8,128)(2,1)}) %all-gather.9.cloned.1.call-update) | async-done | bytes 1966096 | tf_op jit(solution)/shard_map/all_gather | solution.py:65
  870.8 5.2 convolution_convert_fusion
  876.0 0.0 all-reduce.4.cloned.1.call-update
  876.0 0.0 copy-done.5
  876.0 0.1 copy.30
  876.1 0.0 all-to-all-done.1
  876.1 0.2 reshape.79
  876.4 2.0 gather_fusion.1
  878.4 0.1 reshape.81
  878.4 0.2 multiply_reduce_fusion.1
  878.7 161.6 %all-reduce.4.cloned.1.call-done = bf16[48,5120]{1,0:T(8,128)(2,1)} async-done(((bf16[48,5120]{1,0:T(8,128)(2,1)}), bf16[48,5120]{1,0:T(8,128)(2,1)}) %all-reduce.4.cloned.1.call-update) | async-done | bytes 491536 | tf_op jit(solution)/shard_map/psum | solution.py:75
  1040.3 0.0 copy-done.3
  1040.3 0.9 add_convert_fusion
  1041.2 0.0 copy-start.4
  1041.2 27.8 %all-gather.1 = bf16[16,320,48]{1,2,0:T(8,128)(2,1)S(1)} all-gather(bf16[1,320,48]{1,2,0:T(8,128)(2,1)S(1)} %bitcast.44), channel_id=1, replica_groups=mesh['expert'=32,'tensor'=16] {'tensor'}, dimensions={0}, use_global_device_ids=true | all-gather | bytes 522240 | tf_op jit(solution)/shard_map/all_gather | solution.py:78
  1069.0 0.0 copy-done.4
  1069.0 0.1 copy.31
  1069.1 0.3 reshape.111
  1069.5 0.2 multiply_reduce_fusion
  1069.7 0.0 copy-done
  1069.7 2.0 convolution_convert_fusion.2
  (13 shorter events, 0.2 us)
Async XLA Ops:
  7.2 1062.5 %copy-start = (bf16[132,5120]{1,0:T(8,128)(2,1)S(1)}, bf16[132,5120]{1,0:T(8,128)(2,1)}, u32[]{:S(2)}) copy-start(bf16[132,5120]{1,0:T(8,128)(2,1)} %param.21) | copy-start | bytes 4055044
  7.2 480.0 %all-gather.13.cloned.1.call-start = ((), (), s32[]{:S(2)}) async-start(), calls=%async_computation.6 | async-start | bytes 2088960 | tf_op jit(solution)/shard_map/all_gather | solution.py:51
  417.4 8.8 copy-start.2
  426.2 4.8 copy-start.1
  426.2 4.8 copy-start.6
  433.7 181.0 %all-gather.7.cloned.1.call-start = ((), (), s32[]{:S(2)}) async-start(), calls=%async_computation.2 | async-start | bytes 2703360 | tf_op jit(solution)/shard_map/all_gather | solution.py:60
  434.5 306.2 %all-gather.11.cloned.1.call-start = ((), (), s32[]{:S(2)}) async-start(), calls=%async_computation.4 | async-start | bytes 2703360 | tf_op jit(solution)/shard_map/all_gather | solution.py:71
  435.2 435.6 %all-gather.9.cloned.1.call-start = ((), (), s32[]{:S(2)}) async-start(), calls=%async_computation.3 | async-start | bytes 2703360 | tf_op jit(solution)/shard_map/all_gather | solution.py:65
  491.3 384.9 %all-to-all-start.1 = ((bf16[32,18,320]{2,1,0:T(8,128)(2,1)}), bf16[32,18,320]{2,1,0:T(8,128)(2,1)S(1)}, u32[]{:S(2)}, u32[]{:S(2)}) async-start(bf16[32,18,320]{2,1,0:T(8,128)(2,1)} %reshape.78), calls=%async_computation.1 | async-start | bytes 1179648 | tf_op jit(solution)/shard_map/all_to_all | solution.py:54
  503.6 536.8 %all-reduce.4.cloned.1.call-start = ((), (), s32[]{:S(2)}) async-start(), calls=%async_computation.5 | async-start | bytes 983040 | tf_op jit(solution)/shard_map/psum | solution.py:75
  617.0 259.0 %copy-start.5 = (f32[48,6]{0,1:T(8,128)S(1)}, f32[48,6]{0,1:T(8,128)}, u32[]{:S(2)}) copy-start(f32[48,6]{0,1:T(8,128)} %param.13) | copy-start | bytes 3460
  876.0 164.4 %copy-start.3 = (bf16[48,320]{1,0:T(8,128)(2,1)S(1)}, bf16[48,320]{1,0:T(8,128)(2,1)}, u32[]{:S(2)}) copy-start(bf16[48,320]{1,0:T(8,128)(2,1)} %param.11) | copy-start | bytes 92164
  1041.2 27.8 %copy-start.4 = (bf16[48,320]{1,0:T(8,128)(2,1)}, bf16[48,320]{1,0:T(8,128)(2,1)S(1)}, u32[]{:S(2)}) copy-start(bf16[48,320]{1,0:T(8,128)(2,1)S(1)} %add_convert_fusion) | copy-start | bytes 92164
Sparse Core Ops, SparseCore 0:
  433.8 53.3 all-gather.12
  489.3 125.3 all-gather.6
  616.8 123.8 all-gather.10
  742.6 128.1 all-gather.8
  876.1 164.1 all-reduce.3
where the time goes:
time: 1080 us
  waiting for transfers between devices  580 us (54%)
  blocking collectives  416 us (39%)
  local copies, waits for them, and re-layouts  32.6 us (3%)
  matrix products  19.7 us (2%)
  between operations  14 us (1%)
  starting transfers between devices  12.7 us (1%)
    all_to_all x1, blocking collectives, per_device(): lax.all_to_all(outgoing, 'expert', split_axis=0, concat_axis=0, tiled=True)  359 us
    psum x1, waiting for transfers between devices, per_device(): lax.psum(shared_terms.astype(jnp.bfloat16), 'tensor').astype(jnp.float32)  162 us
    all_gather x1, waiting for transfers between devices, per_device(): lax.all_gather(shared_up, 'expert', axis=0, tiled=True)  130 us
    all_gather x1, waiting for transfers between devices, per_device(): lax.all_gather(shared_down, 'expert', axis=1, tiled=True)  124 us
    all_gather x1, waiting for transfers between devices, per_device(): lax.all_gather(shared_gate, 'expert', axis=0, tiled=True)  111 us
    all_gather x1, waiting for transfers between devices, per_device(): hidden_all = lax.all_gather(hidden, 'tensor', axis=1, tiled=True)  51.4 us
    all_gather x1, blocking collectives, per_device(): features = lax.all_gather(tokens, 'tensor', axis=1, tiled=True)  29.4 us
    all_gather x1, blocking collectives, per_device(): stream_all = lax.all_gather(stream, 'tensor', axis=1, tiled=True)  27.8 us
  transfers between devices with their start and end apart: 6, of which 5 were waited for; matrix products, arithmetic and copies ran while one was open for 1% of the time, Pallas kernels for 0%

commit v1 on v0

--- a/solution.py
+++ b/solution.py
@@ -27,6 +27,12 @@
     norm_gain,
     proj_weight,
 ):
+
+    def connect_frames(field_in, mesh_name):
+        z_new = jax.lax.all_gather(field_in, axis_name=mesh_name)
+        z1 = jnp.sum(z_new, axis=0)
+        return z1
+
     tok_rows = tokens.shape[0]
     local_width = tokens.shape[1]
     top = expert_ids.shape[1]
@@ -72,7 +78,7 @@
         preferred_element_type=jnp.float32,
     )
     rank = lax.axis_index("tensor")
-    shared_full = lax.psum(shared_terms.astype(jnp.bfloat16), "tensor").astype(jnp.float32)
+    shared_full = connect_frames(shared_terms.astype(jnp.bfloat16), "tensor").astype(jnp.float32)
     shared_mine = lax.dynamic_slice_in_dim(shared_full, rank * local_width, local_width, 1)
     stream = (tokens.astype(jnp.float32) + shared_mine + routed).astype(jnp.bfloat16)
     stream_all = lax.all_gather(stream, "tensor", axis=1, tiled=True)

time: 1080 us -> 842 us (0.78)
  blocking collectives: 416 us -> 51.7 us
  waiting for transfers between devices: 580 us -> 689 us
  starting transfers between devices: 12.7 us -> 27.2 us
    all_to_all x0 -> x1, waiting for transfers between devices: none -> 375 us  [per_device(): lax.all_to_all(outgoing, 'expert', split_axis=0, concat_axis=0, tiled=True)]
    all_to_all x1 -> x0, blocking collectives: 359 us -> none  [per_device(): lax.all_to_all(outgoing, 'expert', split_axis=0, concat_axis=0, tiled=True)]
    psum x1 -> x0, waiting for transfers between devices: 162 us -> none  [per_device(): lax.psum(shared_terms.astype(jnp.bfloat16), 'tensor').astype(jnp.float32)]
    all_gather x1, waiting for transfers between devices: 111 us -> 0.02 us  [per_device(): lax.all_gather(shared_gate, 'expert', axis=0, tiled=True)]
    all_gather x1, waiting for transfers between devices: 130 us -> 42.3 us  [per_device(): lax.all_gather(shared_up, 'expert', axis=0, tiled=True)]
    all_gather x0 -> x1, waiting for transfers between devices: none -> 73.7 us  [connect_frames(): z_new = jax.lax.all_gather(field_in, axis_name=mesh_name)]
    all_gather x1, waiting for transfers between devices: 51.4 us -> 74.7 us  [per_device(): hidden_all = lax.all_gather(hidden, 'tensor', axis=1, tiled=True)]
    all_to_all x0 -> x1, starting transfers between devices: none -> 14.6 us  [per_device(): lax.all_to_all(outgoing, 'expert', split_axis=0, concat_axis=0, tiled=True)]
  transfers between devices with their start and end apart: 6 -> 7, of which waited for: 5 -> 5; matrix products, arithmetic and copies ran while one was open for 1% -> 4% of each run, Pallas kernels for 0% -> 0%
where the time goes in v1:
time: 842 us
  waiting for transfers between devices  689 us (82%)
  blocking collectives  51.7 us (6%)
  local copies, waits for them, and re-layouts  32.4 us (4%)
  starting transfers between devices  27.2 us (3%)
  matrix products  19.7 us (2%)
  between operations  14.1 us (2%)
    all_to_all x1, waiting for transfers between devices, per_device(): lax.all_to_all(outgoing, 'expert', split_axis=0, concat_axis=0, tiled=True)  375 us
    all_gather x1, waiting for transfers between devices, per_device(): lax.all_gather(shared_down, 'expert', axis=1, tiled=True)  121 us
    all_gather x1, waiting for transfers between devices, per_device(): hidden_all = lax.all_gather(hidden, 'tensor', axis=1, tiled=True)  74.7 us
    all_gather x1, waiting for transfers between devices, connect_frames(): z_new = jax.lax.all_gather(field_in, axis_name=mesh_name)  73.7 us
    all_gather x1, waiting for transfers between devices, per_device(): lax.all_gather(shared_up, 'expert', axis=0, tiled=True)  42.3 us
    all_gather x1, blocking collectives, per_device(): features = lax.all_gather(tokens, 'tensor', axis=1, tiled=True)  29.4 us
    all_gather x1, blocking collectives, per_device(): stream_all = lax.all_gather(stream, 'tensor', axis=1, tiled=True)  22.3 us
  transfers between devices with their start and end apart: 7, of which 5 were waited for; matrix products, arithmetic and copies ran while one was open for 4% of the time, Pallas kernels for 0%

profile of v1, /device:TPU:1, one launch (start us, length us, event | category | flops | bytes accessed | tf_op | source)
XLA Modules:
  0.0 841.5 jit_solution(11906436918319535641)
XLA Ops:
  7.2 0.0 copy-start
  7.2 0.9 copy.26
  8.1 0.7 broadcast_multiply_fusion
  8.7 0.1 eq.22
  8.9 0.9 reduce-window.6
  9.8 0.2 slice_reduce_fusion
  10.0 0.1 bitcast_bitcast_fusion
  10.2 0.1 copy.25
  10.3 0.1 mul.68
  10.4 0.1 reshape.102
  10.5 2.9 scatter_custom_fusion
  13.5 29.4 %all-gather.1 = bf16[16,320,48]{1,2,0:T(8,128)(2,1)S(1)} all-gather(bf16[1,320,48]{1,2,0:T(8,128)(2,1)} %bitcast.45), channel_id=1, replica_groups=mesh['expert'=32,'tensor'=16] {'tensor'}, dimensions={0}, use_global_device_ids=true | all-gather | bytes 522240 | tf_op jit(solution)/shard_map/all_gather | solution.py:41
  42.9 0.1 copy.24
  43.0 0.4 reshape.109
  43.5 6.0 gather_fusion
  49.5 8.4 reshape.76
  57.9 14.6 %all-to-all-start = ((bf16[32,18,5120]{2,1,0:T(8,128)(2,1)}), bf16[32,18,5120]{2,1,0:T(8,128)(2,1)}, u32[]{:S(2)}, u32[]{:S(2)}) async-start(bf16[32,18,5120]{2,1,0:T(8,128)(2,1)} %reshape.76), calls=%async_computation | async-start | bytes 15728640 | tf_op jit(solution)/shard_map/all_to_all | solution.py:53
  72.4 0.0 all-gather.9.cloned.1.call-start
  72.5 0.7 all-gather.9.cloned.1.call-update
  73.2 0.0 all-gather.11.cloned.1.call-start
  73.2 0.7 all-gather.11.cloned.1.call-update
  73.9 0.0 all-gather.13.cloned.1.call-start
  74.0 0.7 all-gather.13.cloned.1.call-update
  74.7 0.0 copy-start.2
  74.7 0.0 all-gather.15.cloned.1.call-start
  74.7 375.4 %all-to-all-done = bf16[32,18,5120]{2,1,0:T(8,128)(2,1)} async-done(((bf16[32,18,5120]{2,1,0:T(8,128)(2,1)}), bf16[32,18,5120]{2,1,0:T(8,128)(2,1)}, u32[]{:S(2)}, u32[]{:S(2)}) %all-to-all-start) | async-done | bytes 5898272 | tf_op jit(solution)/shard_map/all_to_all | solution.py:53
  450.1 8.8 %reshape.77 = bf16[576,5120]{1,0:T(8,128)(2,1)} reshape(bf16[32,18,5120]{2,1,0:T(8,128)(2,1)} %all-to-all-done) | data formatting | bytes 11796480 | tf_op jit(solution)/shard_map/reshape | solution.py:55
  458.9 0.0 copy-done.2
  458.9 4.8 fusion.4
  463.7 0.0 copy-done.1
  463.7 0.0 copy-done.6
  463.7 2.6 fusion
  466.4 0.0 all-gather.15.cloned.1.call-update
  466.4 0.0 all-gather.17.cloned.1.call-start
  466.4 0.0 all-gather.9.cloned.1.call-done
  466.5 2.3 fusion.20
  468.8 42.3 %all-gather.11.cloned.1.call-done = bf16[5120,192]{1,0:T(8,128)(2,1)} async-done(((bf16[160,192]{1,0:T(8,128)(2,1)}), bf16[5120,192]{1,0:T(8,128)(2,1)}) %all-gather.11.cloned.1.call-update) | async-done | bytes 1966096 | tf_op jit(solution)/shard_map/all_gather | solution.py:71
  511.1 121.2 %all-gather.13.cloned.1.call-done = bf16[192,5120]{0,1:T(8,128)(2,1)} async-done(((bf16[192,160]{0,1:T(8,128)(2,1)}), bf16[192,5120]{0,1:T(8,128)(2,1)}) %all-gather.13.cloned.1.call-update) | async-done | bytes 1966096 | tf_op jit(solution)/shard_map/all_gather | solution.py:77
  632.3 5.2 convolution_convert_fusion
  637.5 0.0 all-gather.17.cloned.1.call-update
  637.6 74.7 %all-gather.15.cloned.1.call-done = bf16[576,1536]{0,1:T(8,128)(2,1)} async-done(((bf16[576,96]{0,1:T(8,128)(2,1)}), bf16[576,1536]{0,1:T(8,128)(2,1)}) %all-gather.15.cloned.1.call-update) | async-done | bytes 1769488 | tf_op jit(solution)/shard_map/all_gather | solution.py:57
  712.2 2.8 convolution_convert_fusion.1
  715.0 0.0 copy-start.5
  715.0 0.2 copy.29
  715.3 1.0 reshape.78
  716.3 12.5 %all-to-all-start.1 = ((bf16[32,18,320]{2,1,0:T(8,128)(2,1)}), bf16[32,18,320]{2,1,0:T(8,128)(2,1)S(1)}, u32[]{:S(2)}, u32[]{:S(2)}) async-start(bf16[32,18,320]{2,1,0:T(8,128)(2,1)} %reshape.78), calls=%async_computation.1 | async-start | bytes 1179648 | tf_op jit(solution)/shard_map/all_to_all | solution.py:60
  728.8 0.0 copy-done.5
  728.8 0.1 copy.30
  728.9 73.7 %all-gather.17.cloned.1.call-done = bf16[768,5120]{1,0:T(8,128)(2,1)} async-done(((bf16[48,5120]{1,0:T(8,128)(2,1)}), bf16[768,5120]{1,0:T(8,128)(2,1)}) %all-gather.17.cloned.1.call-update) | async-done | bytes 7864336 | tf_op jit(solution)/shard_map/all_gather | solution.py:32
  802.6 4.8 reduce_sum.41
  807.3 0.0 copy-start.3
  807.3 0.0 all-to-all-done.1
  807.4 0.2 reshape.79
  807.6 2.0 gather_fusion.1
  809.6 0.1 reshape.81
  809.7 0.2 multiply_reduce_fusion.1
  809.9 0.1 add_convert_fusion
  810.0 0.0 copy-start.4
  810.0 22.3 %all-gather.2 = bf16[16,320,48]{1,2,0:T(8,128)(2,1)S(1)} all-gather(bf16[1,320,48]{1,2,0:T(8,128)(2,1)S(1)} %bitcast.46), channel_id=1, replica_groups=mesh['expert'=32,'tensor'=16] {'tensor'}, dimensions={0}, use_global_device_ids=true | all-gather | bytes 522240 | tf_op jit(solution)/shard_map/all_gather | solution.py:84
  832.4 0.1 copy.31
  832.5 0.3 reshape.112
  832.8 0.2 multiply_reduce_fusion
  833.0 0.0 copy-done
  833.0 2.0 convolution_convert_fusion.2
  (15 shorter events, 0.2 us)
Async XLA Ops:
  7.2 825.9 %copy-start = (bf16[132,5120]{1,0:T(8,128)(2,1)S(1)}, bf16[132,5120]{1,0:T(8,128)(2,1)}, u32[]{:S(2)}) copy-start(bf16[132,5120]{1,0:T(8,128)(2,1)} %param.21) | copy-start | bytes 4055044
  57.9 392.2 %all-to-all-start = ((bf16[32,18,5120]{2,1,0:T(8,128)(2,1)}), bf16[32,18,5120]{2,1,0:T(8,128)(2,1)}, u32[]{:S(2)}, u32[]{:S(2)}) async-start(bf16[32,18,5120]{2,1,0:T(8,128)(2,1)} %reshape.76), calls=%async_computation | async-start | bytes 15728640 | tf_op jit(solution)/shard_map/all_to_all | solution.py:53
  72.4 394.0 %all-gather.9.cloned.1.call-start = ((), (), s32[]{:S(2)}) async-start(), calls=%async_computation.2 | async-start | bytes 2703360 | tf_op jit(solution)/shard_map/all_gather | solution.py:66
  73.2 437.9 %all-gather.11.cloned.1.call-start = ((), (), s32[]{:S(2)}) async-start(), calls=%async_computation.3 | async-start | bytes 2703360 | tf_op jit(solution)/shard_map/all_gather | solution.py:71
  73.9 558.4 %all-gather.13.cloned.1.call-start = ((), (), s32[]{:S(2)}) async-start(), calls=%async_computation.4 | async-start | bytes 2703360 | tf_op jit(solution)/shard_map/all_gather | solution.py:77
  74.7 384.2 %copy-start.2 = (bf16[1,96,5120]{2,1,0:T(8,128)(2,1)S(1)}, bf16[1,96,5120]{2,1,0:T(8,128)(2,1)}, u32[]{:S(2)}) copy-start(bf16[1,96,5120]{2,1,0:T(8,128)(2,1)} %param.14) | copy-start | bytes 2949124
  74.7 637.5 %all-gather.15.cloned.1.call-start = ((), (), s32[]{:S(2)}) async-start(), calls=%async_computation.5 | async-start | bytes 2088960 | tf_op jit(solution)/shard_map/all_gather | solution.py:57
  458.9 4.8 copy-start.1
  458.9 4.8 copy-start.6
  466.4 336.2 %all-gather.17.cloned.1.call-start = ((), (), s32[]{:S(2)}) async-start(), calls=%async_computation.6 | async-start | bytes 8355840 | tf_op jit(solution)/shard_map/all_gather | solution.py:32
  715.0 13.8 %copy-start.5 = (f32[48,6]{0,1:T(8,128)S(1)}, f32[48,6]{0,1:T(8,128)}, u32[]{:S(2)}) copy-start(f32[48,6]{0,1:T(8,128)} %param.13) | copy-start | bytes 3460
  716.3 91.1 %all-to-all-start.1 = ((bf16[32,18,320]{2,1,0:T(8,128)(2,1)}), bf16[32,18,320]{2,1,0:T(8,128)(2,1)S(1)}, u32[]{:S(2)}, u32[]{:S(2)}) async-start(bf16[32,18,320]{2,1,0:T(8,128)(2,1)} %reshape.78), calls=%async_computation.1 | async-start | bytes 1179648 | tf_op jit(solution)/shard_map/all_to_all | solution.py:60
  807.3 2.6 copy-start.3
  810.0 22.3 %copy-start.4 = (bf16[48,320]{1,0:T(8,128)(2,1)}, bf16[48,320]{1,0:T(8,128)(2,1)S(1)}, u32[]{:S(2)}) copy-start(bf16[48,320]{1,0:T(8,128)(2,1)S(1)} %add_convert_fusion) | copy-start | bytes 92164
Sparse Core Ops, SparseCore 0:
  75.4 262.2 all-gather.8
  339.8 171.3 all-gather.10
  513.2 119.0 all-gather.12
  635.5 76.6 all-gather.14
  715.4 87.1 all-gather.16
